TPU v7x, 512 devices: a whole 4x8x8 slice. The times are simulated.
512 devices in a mesh: dom: 64 (over x, y, core), ch: 8 (over z).
Axes of the slice: x: 4, y: 8, z: 8, core: 2. Of those that a mesh axis runs over, the one named last changes fastest.
Arguments:
- features: bfloat16 [25, 128, 98304], P(None, 'ch', 'dom'), may hold values from -6 to 6
- neighbours: int32 [32, 32768], P(None, 'dom'), may hold values from 0 to 98303, as said below
- pad_mask: int32 [32, 32768], P(None, 'dom'), may hold values 0 or 1
- displacement: float32 [3, 32, 32768], P(None, None, 'dom'), may hold values from -1.5 to 1.5
- radial_weight: float32 [8, 5, 128], P(None, None, 'ch'), may hold values from -2 to 2
- mixing_weight: bfloat16 [128, 128], replicated, may hold values from -0.5 to 0.5
- readout_weight: float32 [128], P('ch'), may hold values from -0.5 to 0.5
Outputs:
- density: float32 [32768], P('dom')
Inputs may be any that keep to these rules, and one draw needn't show every extreme that they name: `neighbours`: atom a lies in domain a // 1536 and probe p in brick p // 512; every neighbour of a probe lies in the domain of the probe's brick or in one of the two domains on either side of it, counted cyclically over the 64 domains.
All inputs are finite; a program needn't handle non-finite values. No bound on the sum of `pad_mask` on one device may be relied on, other than what follows from the above.
Results may differ from a plain program's by a relative error of at most 0.0003.
Values may be sent and summed in bfloat16 or wider, within the bound.
A program may use at most 64 MiB of HBM per device.

v0:
```python
import jax
import jax.numpy as jnp
from jax import lax
from jax.sharding import PartitionSpec as P

degree_bounds = ((0, 1), (1, 4), (4, 9), (9, 16), (16, 25))


def shifted(value, axis, steps):
    count = lax.axis_size(axis)
    pairs = [(source, (source + steps) % count) for source in range(count)]
    return lax.ppermute(value, axis, pairs)


def harmonics(coords):
    coord_x, coord_y, coord_z = (coords[0], coords[1], coords[2])
    square_x = coord_x * coord_x
    square_y = coord_y * coord_y
    square_z = coord_z * coord_z
    radius_sq = square_x + square_y + square_z
    components = [
        jnp.ones_like(coord_x),
        coord_x,
        coord_y,
        coord_z,
        coord_x * coord_y,
        coord_y * coord_z,
        (3.0 * square_z - radius_sq) * 0.2887,
        coord_x * coord_z,
        0.5 * (square_x - square_y),
        coord_y * (3.0 * square_x - square_y) * 0.2,
        coord_x * coord_y * coord_z,
        coord_y * (4.0 * square_z - square_x - square_y) * 0.15,
        coord_z * (2.0 * square_z - 3.0 * square_x - 3.0 * square_y) * 0.15,
        coord_x * (4.0 * square_z - square_x - square_y) * 0.15,
        0.5 * coord_z * (square_x - square_y),
        coord_x * (square_x - 3.0 * square_y) * 0.2,
        coord_x * coord_y * (square_x - square_y) * 0.5,
        coord_y * coord_z * (3.0 * square_x - square_y) * 0.2,
        coord_x * coord_y * (7.0 * square_z - radius_sq) * 0.1,
        coord_y * coord_z * (7.0 * square_z - 3.0 * radius_sq) * 0.1,
        (35.0 * square_z * square_z - 30.0 * square_z * radius_sq + 3.0 * radius_sq * radius_sq)
        * 0.02,
        coord_x * coord_z * (7.0 * square_z - 3.0 * radius_sq) * 0.1,
        (square_x - square_y) * (7.0 * square_z - radius_sq) * 0.05,
        coord_x * coord_z * (square_x - 3.0 * square_y) * 0.2,
        (square_x * square_x - 6.0 * square_x * square_y + square_y * square_y) * 0.1,
    ]
    return jnp.stack(components)


def gaussians_of(coords, count_basis):
    radius_sq = coords[0] * coords[0] + coords[1] * coords[1] + coords[2] * coords[2]
    centers = 0.9 * jnp.arange(count_basis, dtype=jnp.float32)
    spread = radius_sq[None] - centers.reshape((count_basis,) + (1,) * radius_sq.ndim)
    return jnp.exp(-(spread * spread))


def fetch_window(features, offset):
    return shifted(features, "dom", -offset)


def pair_sum(table, slot_index, slot_use, displacement, radial_weight):
    comp_count = table.shape[0]
    chan_local = table.shape[1]
    table_rows = jnp.moveaxis(table, 2, 0).reshape(table.shape[2], comp_count * chan_local)
    slot_count = slot_index.shape[0]
    probe_count = slot_index.shape[1]
    block_size = min(256, probe_count)
    count_blocks = probe_count // block_size
    index_blocks = jnp.moveaxis(slot_index.reshape(slot_count, count_blocks, block_size), 1, 0)
    use_blocks = jnp.moveaxis(slot_use.reshape(slot_count, count_blocks, block_size), 1, 0)
    disp_blocks = jnp.moveaxis(displacement.reshape(3, slot_count, count_blocks, block_size), 2, 0)

    def one_block(inputs):
        index_block, use_block, disp_block = inputs
        pair_count = slot_count * block_size
        pair_disp = jnp.swapaxes(disp_block, 1, 2).reshape(3, pair_count)
        pair_index = index_block.T.reshape(pair_count)
        pair_use = use_block.T.reshape(pair_count, 1).astype(jnp.float32)
        harmonic = harmonics(pair_disp).T
        gaussian = gaussians_of(pair_disp, radial_weight.shape[0]).T
        gathered = jnp.take(table_rows, pair_index, axis=0).reshape(
            pair_count, comp_count, chan_local
        )
        summed = jnp.zeros((pair_count, chan_local), jnp.float32)
        for degree in range(5):
            first_comp, last_comp = degree_bounds[degree]
            projection = jnp.sum(
                gathered[:, first_comp:last_comp, :] * harmonic[:, first_comp:last_comp, None],
                axis=1,
            )
            radial_part = jnp.dot(
                gaussian, radial_weight[:, degree, :], precision=lax.Precision.HIGHEST
            )
            summed = summed + radial_part * projection
        summed = summed * pair_use
        return jnp.sum(summed.reshape(block_size, slot_count, chan_local), axis=1) * (
            1.0 / slot_count
        )

    results = lax.map(one_block, (index_blocks, use_blocks, disp_blocks))
    return results.reshape(probe_count, chan_local).T


def per_device(
    features, neighbours, pad_mask, displacement, radial_weight, mixing_weight, readout_weight
):
    atom_count = features.shape[2]
    chan_local = features.shape[1]
    count_dom = lax.axis_size("dom")
    my_domain = lax.axis_index("dom")
    domain = neighbours // atom_count
    distance = (domain - my_domain + count_dom) % count_dom
    offset = jnp.where(distance > count_dom // 2, distance - count_dom, distance)
    local_atom = neighbours % atom_count
    received = [fetch_window(features, step_offset) for step_offset in (-2, -1, 1, 2)]
    window_table = jnp.concatenate(
        [received[0], received[1], features, received[2], received[3]], axis=2
    )
    slot_index = (offset + 2) * atom_count + local_atom
    field_sum = pair_sum(window_table, slot_index, pad_mask, displacement, radial_weight)
    my_slice = lax.axis_index("ch")
    mixing_full = mixing_weight.astype(jnp.float32)
    weight_rows = lax.dynamic_slice_in_dim(mixing_full, my_slice * chan_local, chan_local, 0)
    mixed_channels = lax.psum_scatter(
        jnp.dot(weight_rows.T, field_sum, precision=lax.Precision.HIGHEST),
        "ch",
        scatter_dimension=0,
        tiled=True,
    )
    partial_density = jnp.sum(readout_weight[:, None] * jax.nn.silu(mixed_channels), axis=0)
    return lax.psum(partial_density, "ch")


def solution(mesh):
    return jax.shard_map(
        per_device,
        mesh=mesh,
        in_specs=(
            P(None, "ch", "dom"),
            P(None, "dom"),
            P(None, "dom"),
            P(None, None, "dom"),
            P(None, None, "ch"),
            P(),
            P("ch"),
        ),
        out_specs=P("dom"),
        check_vma=False,
    )
```

profile of v0, /device:TPU:2, one launch (start us, length us, event | category | flops | bytes accessed | tf_op | source)
XLA Modules:
  0.0 304.1 jit_solution(2592125997334953614)
XLA Ops:
  6.5 3.6 %collective-permute-start = (bf16[25,16,1536]{2,1,0:T(8,128)(2,1)}, bf16[25,16,1536]{2,1,0:T(8,128)(2,1)}, u32[]{:S(2)}, u32[]{:S(2)}) collective-permute-start(bf16[25,16,1536]{2,1,0:T(8,128)(2,1)} %param.9), channel_id=1, source_target_pairs={{0,16},{8,24},{16,32},{24,40},{32,48},{40,56},{48,64},{56,72},{64,... | collective-permute-start | bytes 3686408 | tf_op jit(solution)/shard_map/ppermute | solution.py:12
  10.2 1.9 collective-permute-start.1
  12.1 5.8 %collective-permute-start.2 = (bf16[25,16,1536]{2,1,0:T(8,128)(2,1)}, bf16[25,16,1536]{2,1,0:T(8,128)(2,1)}, u32[]{:S(2)}, u32[]{:S(2)}) collective-permute-start(bf16[25,16,1536]{2,1,0:T(8,128)(2,1)} %param.9), channel_id=1, source_target_pairs={{0,504},{8,0},{16,8},{24,16},{32,24},{40,32},{48,40},{56,48},{64,5... | collective-permute-start | bytes 3686408 | tf_op jit(solution)/shard_map/ppermute | solution.py:12
  17.8 2.4 collective-permute-start.3
  20.2 1.7 reshape.637
  23.6 1.5 reshape.640
  25.1 15.8 %collective-permute-done = bf16[25,16,1536]{2,1,0:T(8,128)(2,1)} collective-permute-done((bf16[25,16,1536]{2,1,0:T(8,128)(2,1)}, bf16[25,16,1536]{2,1,0:T(8,128)(2,1)}, u32[]{:S(2)}, u32[]{:S(2)}) %collective-permute-start) | collective-permute-done | bytes 1228832 | tf_op jit(solution)/shard_map/ppermute | solution.py:12
  40.9 2.4 constant_dynamic-update-slice_fusion.4
  43.3 9.6 %collective-permute-done.1 = bf16[25,16,1536]{2,1,0:T(8,128)(2,1)} collective-permute-done((bf16[25,16,1536]{2,1,0:T(8,128)(2,1)}, bf16[25,16,1536]{2,1,0:T(8,128)(2,1)}, u32[]{:S(2)}, u32[]{:S(2)}) %collective-permute-start.1) | collective-permute-done | bytes 1228832 | tf_op jit(solution)/shard_map/ppermute | solution.py:12
  52.9 2.5 constant_dynamic-update-slice_fusion.3
  55.4 1.2 constant_dynamic-update-slice_fusion.2
  56.6 2.5 constant_dynamic-update-slice_fusion.1
  59.1 1.1 constant_dynamic-update-slice_fusion
  60.2 9.7 %copy.13 = bf16[7680,400]{1,0:T(8,128)(2,1)} copy(bf16[7680,400]{0,1:T(8,128)(2,1)} %bitcast.22) | data formatting | bytes 12288000 | tf_op jit(solution)/shard_map/while | solution.py:102
  69.9 164.6 %while.10 = (s32[]{:T(128)}, f32[2,256,16]{1,0,2:T(2,128)}, f32[2,3,32,256]{3,0,2,1:T(2,128)}, f32[8,5,16]{2,0,1:T(8,128)}, s32[2,32,256]{2,0,1:T(2,128)}, /*ind...) while((s32[]{:T(128)}, f32[2,256,16]{1,0,2:T(2,128)}, ...), condition=%wide.region_6.7_spmd, body=%wide.region_0.6_spmd.sunk | while | flops 78585864 | bytes 83885984 | solution.py:102
  69.9 1.6 constant_dynamic-slice_fusion.5
  71.8 38.0 %gather_fusion = bf16[8192,400]{1,0:T(8,128)(2,1)} fusion(bf16[7680,400]{1,0:T(8,128)(2,1)} %get-tuple-element.235, s32[8192]{0:T(1024)S(1)} %broadcast_clamp_fusion.2), kind=kCustom, calls=%fused_computation.clone.1 | custom fusion | bytes 13139968 | tf_op jit(solution)/shard_map/while/body/eval_jaxpr/jit(_take)/gather | solution.py:83
  109.8 10.7 %copy.29 = bf16[8192,400]{0,1:T(8,128)(2,1)} copy(bf16[8192,400]{1,0:T(8,128)(2,1)} %gather_fusion) | data formatting | bytes 13107200 | tf_op jit(solution)/shard_map/while/body/eval_jaxpr/jit(_take)/gather | solution.py:83
  120.6 6.3 %broadcast_select_fusion.2 = bf16[8192,25,16]{0,2,1:T(8,128)(2,1)} fusion(bf16[8192,25,16]{0,2,1:T(8,128)(2,1)} %bitcast.74, pred[8192]{0:T(1024)(128)(4,1)S(1)} %compare_and_fusion.2), kind=kLoop, calls=%fused_computation.11.clone.1 | loop fusion | flops 3276800 | bytes 13115392 | tf_op jit(solution)/shard_map/while/body/eval_jaxpr/jit(_take)/select_n | solution.py:83
  126.9 1.0 constant_dynamic-slice_fusion.6
  130.1 1.2 multiply_multiply_fusion.19
  132.7 4.5 %stack.3 = f32[25,8192]{1,0:T(8,128)S(1)} concatenate(f32[1,8192]{1,0:T(1,128)} %broadcast.428, f32[1,8192]{1,0:T(1,128)S(1)} %squeeze.42, f32[1,8192]{1,0:T(1,128)S(1)} %squeeze.43, f32[1,8192]{1,0:T(1,128)S(1)} %squeeze.44, f32[1,8192]{1,0:T(1,128)} %copy-done.1, f32[1,8192]{1,0:T(1,128)} %copy-done.2, f32[1,8192]{1,0:T(1,128)} %get-tuple-element.188, f32[1,8192]{1,0:T(1,128)} %copy-done.3, ...), dimensions={0} | concatenate | bytes 1638400 | tf_op jit(solution)/shard_map/while/body/eval_jaxpr/stack | solution.py:49
  137.2 1.0 add.245
  138.2 1.6 convolution_multiply_fusion.6
  139.9 1.5 multiply_reduce_fusion.9
  141.4 1.3 fusion.53
  142.8 1.7 multiply_reduce_fusion.10
  145.6 1.4 fusion.55
  147.8 1.7 fusion.56
  150.8 1.4 dynamic_update_slice.5
  152.3 1.5 constant_dynamic-slice_fusion.5
  154.1 38.0 %gather_fusion = bf16[8192,400]{1,0:T(8,128)(2,1)} fusion(bf16[7680,400]{1,0:T(8,128)(2,1)} %get-tuple-element.235, s32[8192]{0:T(1024)S(1)} %broadcast_clamp_fusion.2), kind=kCustom, calls=%fused_computation.clone.1 | custom fusion | bytes 13139968 | tf_op jit(solution)/shard_map/while/body/eval_jaxpr/jit(_take)/gather | solution.py:83
  192.1 10.7 %copy.29 = bf16[8192,400]{0,1:T(8,128)(2,1)} copy(bf16[8192,400]{1,0:T(8,128)(2,1)} %gather_fusion) | data formatting | bytes 13107200 | tf_op jit(solution)/shard_map/while/body/eval_jaxpr/jit(_take)/gather | solution.py:83
  202.9 6.3 %broadcast_select_fusion.2 = bf16[8192,25,16]{0,2,1:T(8,128)(2,1)} fusion(bf16[8192,25,16]{0,2,1:T(8,128)(2,1)} %bitcast.74, pred[8192]{0:T(1024)(128)(4,1)S(1)} %compare_and_fusion.2), kind=kLoop, calls=%fused_computation.11.clone.1 | loop fusion | flops 3276800 | bytes 13115392 | tf_op jit(solution)/shard_map/while/body/eval_jaxpr/jit(_take)/select_n | solution.py:83
  209.2 1.0 constant_dynamic-slice_fusion.6
  212.4 1.2 multiply_multiply_fusion.19
  215.0 4.5 %stack.3 = f32[25,8192]{1,0:T(8,128)S(1)} concatenate(f32[1,8192]{1,0:T(1,128)} %broadcast.428, f32[1,8192]{1,0:T(1,128)S(1)} %squeeze.42, f32[1,8192]{1,0:T(1,128)S(1)} %squeeze.43, f32[1,8192]{1,0:T(1,128)S(1)} %squeeze.44, f32[1,8192]{1,0:T(1,128)} %copy-done.1, f32[1,8192]{1,0:T(1,128)} %copy-done.2, f32[1,8192]{1,0:T(1,128)} %get-tuple-element.188, f32[1,8192]{1,0:T(1,128)} %copy-done.3, ...), dimensions={0} | concatenate | bytes 1638400 | tf_op jit(solution)/shard_map/while/body/eval_jaxpr/stack | solution.py:49
  219.5 1.0 add.245
  220.5 1.6 convolution_multiply_fusion.6
  222.2 1.5 multiply_reduce_fusion.9
  223.7 1.3 fusion.53
  225.1 1.7 multiply_reduce_fusion.10
  227.9 1.4 fusion.55
  230.1 1.7 fusion.56
  233.2 1.4 dynamic_update_slice.5
  235.3 1.0 fusion.35
  236.4 44.1 %reduce-scatter.2.cloned.1.call-done = f32[16,512]{1,0:T(8,128)} async-done(((f32[128,512]{1,0:T(8,128)}), f32[16,512]{1,0:T(8,128)}) %reduce-scatter.2.cloned.1.call-update) | async-done | bytes 32784 | tf_op jit(solution)/shard_map/reduce_scatter | solution.py:126
  281.3 15.9 %psum.7 = f32[512]{0:T(512)} all-reduce(f32[512]{0:T(512)S(1)} %multiply_reduce_fusion.4), channel_id=1, replica_groups=mesh['dom'=64,'ch'=8] {'ch'}, use_global_device_ids=true, to_apply=%region_9.10 | all-reduce | flops 512 | bytes 4096 | tf_op jit(solution)/shard_map/psum | solution.py:133
  (105 shorter events, 17.6 us)
Async XLA Ops:
  6.5 228.8 %copy-start = (bf16[128,128]{1,0:T(8,128)(2,1)S(1)}, bf16[128,128]{1,0:T(8,128)(2,1)}, u32[]{:S(2)}) copy-start(bf16[128,128]{1,0:T(8,128)(2,1)} %param.14) | copy-start | bytes 98308
  6.5 48.9 %copy-start.5 = (bf16[25,16,1536]{2,1,0:T(8,128)(2,1)S(1)}, bf16[25,16,1536]{2,1,0:T(8,128)(2,1)}, u32[]{:S(2)}) copy-start(bf16[25,16,1536]{2,1,0:T(8,128)(2,1)} %param.9) | copy-start | bytes 3686404
  6.5 273.9 %reduce-scatter.2.cloned.1.call-start = ((), (), s32[]{:S(2)}) async-start(), calls=%async_computation.1 | async-start | bytes 294912 | tf_op jit(solution)/shard_map/reduce_scatter | solution.py:126
  6.5 34.3 %collective-permute-start = (bf16[25,16,1536]{2,1,0:T(8,128)(2,1)}, bf16[25,16,1536]{2,1,0:T(8,128)(2,1)}, u32[]{:S(2)}, u32[]{:S(2)}) collective-permute-start(bf16[25,16,1536]{2,1,0:T(8,128)(2,1)} %param.9), channel_id=1, source_target_pairs={{0,16},{8,24},{16,32},{24,40},{32,48},{40,56},{48,64},{56,72},{64,... | collective-permute-start | bytes 3686408 | tf_op jit(solution)/shard_map/ppermute | solution.py:12
  10.2 42.8 %collective-permute-start.1 = (bf16[25,16,1536]{2,1,0:T(8,128)(2,1)}, bf16[25,16,1536]{2,1,0:T(8,128)(2,1)}, u32[]{:S(2)}, u32[]{:S(2)}) collective-permute-start(bf16[25,16,1536]{2,1,0:T(8,128)(2,1)} %param.9), channel_id=1, source_target_pairs={{0,8},{8,16},{16,24},{24,32},{32,40},{40,48},{48,56},{56,64},{64,7... | collective-permute-start | bytes 3686408 | tf_op jit(solution)/shard_map/ppermute | solution.py:12
  12.1 44.5 %collective-permute-start.2 = (bf16[25,16,1536]{2,1,0:T(8,128)(2,1)}, bf16[25,16,1536]{2,1,0:T(8,128)(2,1)}, u32[]{:S(2)}, u32[]{:S(2)}) collective-permute-start(bf16[25,16,1536]{2,1,0:T(8,128)(2,1)} %param.9), channel_id=1, source_target_pairs={{0,504},{8,0},{16,8},{24,16},{32,24},{40,32},{48,40},{56,48},{64,5... | collective-permute-start | bytes 3686408 | tf_op jit(solution)/shard_map/ppermute | solution.py:12
  17.8 41.2 %collective-permute-start.3 = (bf16[25,16,1536]{2,1,0:T(8,128)(2,1)}, bf16[25,16,1536]{2,1,0:T(8,128)(2,1)S(1)}, u32[]{:S(2)}, u32[]{:S(2)}) collective-permute-start(bf16[25,16,1536]{2,1,0:T(8,128)(2,1)} %param.9), channel_id=1, source_target_pairs={{0,496},{8,504},{16,0},{24,8},{32,16},{40,24},{48,32},{56,40},{64,... | collective-permute-start | bytes 3686408 | tf_op jit(solution)/shard_map/ppermute | solution.py:12
  69.9 210.5 %copy-start.7 = (f32[16]{0:T(128)S(1)}, f32[16]{0:T(128)}, u32[]{:S(2)}) copy-start(f32[16]{0:T(128)} %param.15) | copy-start | bytes 196
  128.8 16.4 %slice-start = ((s8[6553600]{0:T(1024)(128)(4,1)}), s8[2359296]{0:T(1024)(128)(4,1)S(1)}, s32[]{:S(2)}) async-start(s8[6553600]{0:T(1024)(128)(4,1)} %bitcast.75), calls=%async_computation.2 | async-start | bytes 4718592 | tf_op jit(solution)/shard_map/while
  130.1 2.0 copy-start.3
  131.3 0.8 copy-start.1
  131.3 0.8 copy-start.2
  137.2 7.3 %copy-start.6 = (f32[8,5,16]{2,0,1:T(8,128)S(1)}, f32[8,5,16]{2,0,1:T(8,128)}, u32[]{:S(2)}) copy-start(f32[8,5,16]{2,0,1:T(8,128)} %get-tuple-element.233) | copy-start | bytes 7684 | tf_op jit(solution)/shard_map/while
  139.9 5.3 %slice-start.1 = ((s8[6553600]{0:T(1024)(128)(4,1)}), s8[4194304]{0:T(1024)(128)(4,1)S(1)}, s32[]{:S(2)}) async-start(s8[6553600]{0:T(1024)(128)(4,1)} %bitcast.75), calls=%async_computation.3 | async-start | bytes 8388608 | tf_op jit(solution)/shard_map/while
  142.8 4.8 %copy-start.4 = (s32[1,32,256]{2,0,1:T(1,128)S(1)}, s32[1,32,256]{2,0,1:T(1,128)}, u32[]{:S(2)}) copy-start(s32[1,32,256]{2,0,1:T(1,128)} %get-tuple-element.207) | copy-start | bytes 98308 | tf_op jit(solution)/shard_map/while
  211.1 16.4 %slice-start = ((s8[6553600]{0:T(1024)(128)(4,1)}), s8[2359296]{0:T(1024)(128)(4,1)S(1)}, s32[]{:S(2)}) async-start(s8[6553600]{0:T(1024)(128)(4,1)} %bitcast.75), calls=%async_computation.2 | async-start | bytes 4718592 | tf_op jit(solution)/shard_map/while
  212.4 2.0 copy-start.3
  213.6 0.8 copy-start.1
  213.6 0.8 copy-start.2
  219.5 7.3 %copy-start.6 = (f32[8,5,16]{2,0,1:T(8,128)S(1)}, f32[8,5,16]{2,0,1:T(8,128)}, u32[]{:S(2)}) copy-start(f32[8,5,16]{2,0,1:T(8,128)} %get-tuple-element.233) | copy-start | bytes 7684 | tf_op jit(solution)/shard_map/while
  222.2 5.3 %slice-start.1 = ((s8[6553600]{0:T(1024)(128)(4,1)}), s8[4194304]{0:T(1024)(128)(4,1)S(1)}, s32[]{:S(2)}) async-start(s8[6553600]{0:T(1024)(128)(4,1)} %bitcast.75), calls=%async_computation.3 | async-start | bytes 8388608 | tf_op jit(solution)/shard_map/while
  225.1 4.8 %copy-start.4 = (s32[1,32,256]{2,0,1:T(1,128)S(1)}, s32[1,32,256]{2,0,1:T(1,128)}, u32[]{:S(2)}) copy-start(s32[1,32,256]{2,0,1:T(1,128)} %get-tuple-element.207) | copy-start | bytes 98308 | tf_op jit(solution)/shard_map/while
Sparse Core Ops, SparseCore 0:
  236.5 43.8 reduce-scatter.1
where the time goes:
time: 307 us; the launch traced here: 304 us
  local copies, waits for them, and re-layouts  145 us (47%)
  waiting for transfers between devices  69.5 us (23%)
  other arithmetic  31.1 us (10%)
  blocking collectives  15.9 us (5%)
  matrix products  14.5 us (5%)
  starting transfers between devices  13.6 us (4%)
  between operations  13.4 us (4%)
    gather x4, local copies, waits for them, and re-layouts, one_block(): jnp.take(table_rows, pair_index, axis=0)  97.4 us
    reduce_scatter x1, waiting for transfers between devices, per_device(): lax.psum_scatter(jnp.dot(weight_rows.T, field_sum, precision=lax.Precisio...  44.1 us
    ppermute x4, waiting for transfers between devices, shifted(): return lax.ppermute(value, axis, pairs)  25.4 us
    psum x1, blocking collectives, per_device(): return lax.psum(partial_density, 'ch')  15.9 us
    ppermute x4, starting transfers between devices, shifted(): return lax.ppermute(value, axis, pairs)  13.6 us
    dot_general x10, matrix products, one_block(): jnp.dot(gaussian, radial_weight[:, degree, :], precision=lax.Precision.HI...  13.5 us
    select_n x4, other arithmetic, one_block(): jnp.take(table_rows, pair_index, axis=0)  12.6 us
    while x1, local copies, waits for them, and re-layouts, pair_sum(): results = lax.map(one_block, (index_blocks, use_blocks, disp_blocks))  9.71 us
  transfers between devices with their start and end apart: 5, of which 3 were waited for; matrix products, arithmetic and copies ran while one was open for 4% of the time, Pallas kernels for 0%

commit v1 on v0

v1 whole, which is shorter than its diff:
```python
import functools

import jax
import jax.numpy as jnp
from jax import lax
from jax.experimental import pallas as pl
from jax.experimental.pallas import tpu as pltpu
from jax.sharding import PartitionSpec as P

COMPS = 25
CHAN = 16
ROWS = COMPS * CHAN
ATOMS = 1536
PROBES = 512
SLOTS = 32
BASIS = 8
WINDOWS = 5
CHUNK = 256
CHUNKS = ATOMS // CHUNK
HALF = CHUNKS // 2
PAD = 4
TABLE_ROWS = PAD + WINDOWS * ATOMS * 4 + PAD
SLOT_ROWS = PROBES * 4
PEERS = 8
UNROLL = 4
DEGREES = ((0, 1), (1, 4), (4, 9), (9, 16), (16, 25))
MESH = pl.DeviceIdType.MESH
f32 = jnp.float32
bf16 = jnp.bfloat16


def harmonics(coord_x, coord_y, coord_z):
    square_x = coord_x * coord_x
    square_y = coord_y * coord_y
    square_z = coord_z * coord_z
    radius_sq = square_x + square_y + square_z
    components = [
        jnp.ones_like(coord_x),
        coord_x,
        coord_y,
        coord_z,
        coord_x * coord_y,
        coord_y * coord_z,
        (3.0 * square_z - radius_sq) * 0.2887,
        coord_x * coord_z,
        0.5 * (square_x - square_y),
        coord_y * (3.0 * square_x - square_y) * 0.2,
        coord_x * coord_y * coord_z,
        coord_y * (4.0 * square_z - square_x - square_y) * 0.15,
        coord_z * (2.0 * square_z - 3.0 * square_x - 3.0 * square_y) * 0.15,
        coord_x * (4.0 * square_z - square_x - square_y) * 0.15,
        0.5 * coord_z * (square_x - square_y),
        coord_x * (square_x - 3.0 * square_y) * 0.2,
        coord_x * coord_y * (square_x - square_y) * 0.5,
        coord_y * coord_z * (3.0 * square_x - square_y) * 0.2,
        coord_x * coord_y * (7.0 * square_z - radius_sq) * 0.1,
        coord_y * coord_z * (7.0 * square_z - 3.0 * radius_sq) * 0.1,
        (35.0 * square_z * square_z - 30.0 * square_z * radius_sq + 3.0 * radius_sq * radius_sq)
        * 0.02,
        coord_x * coord_z * (7.0 * square_z - 3.0 * radius_sq) * 0.1,
        (square_x - square_y) * (7.0 * square_z - radius_sq) * 0.05,
        coord_x * coord_z * (square_x - 3.0 * square_y) * 0.2,
        (square_x * square_x - 6.0 * square_x * square_y + square_y * square_y) * 0.1,
    ]
    return components, radius_sq


def iota(shape, dim):
    return lax.broadcasted_iota(jnp.int32, shape, dim)


def split3(value):
    first = value.astype(bf16)
    rest = value - first.astype(f32)
    second = rest.astype(bf16)
    third = (rest - second.astype(f32)).astype(bf16)
    return first, second, third


def dot(left, right, left_dim, right_dim):
    return lax.dot_general(
        left, right, (((left_dim,), (right_dim,)), ((), ())), preferred_element_type=f32
    )


def kernel(
    feat,
    nbr_hbm,
    mask_hbm,
    disp_hbm,
    radial_hbm,
    mixing_hbm,
    readout_hbm,
    out,
    nbr,
    mask,
    disp,
    radial,
    mixing,
    readout,
    win,
    table,
    weights,
    acc,
    feats,
    expand,
    idx_vmem,
    field_all,
    send_read,
    recv_read,
    input_sem,
    win_send,
    win_recv,
    fwd_send,
    own_sem,
    idx_sem,
    peer_send,
    peer_recv,
    *idx,
):
    me = lax.axis_index("dom")
    my_ch = lax.axis_index("ch")
    count = lax.axis_size("dom")
    odd = lax.rem(me, 2)

    def at(offset):
        return lax.rem(me + offset + count, count)

    barrier = pltpu.get_barrier_semaphore()
    for offset in (-2, -1, 1, 2):
        pl.semaphore_signal(barrier, inc=1, device_id={"dom": at(offset)}, device_id_type=MESH)
    for step in range(1, PEERS):
        peer = lax.rem(my_ch + step, PEERS)
        pl.semaphore_signal(barrier, inc=1, device_id={"ch": peer}, device_id_type=MESH)

    input_copies = [
        pltpu.make_async_copy(source, landing, input_sem.at[place])
        for place, (source, landing) in enumerate(
            (
                (nbr_hbm, nbr),
                (mask_hbm, mask),
                (disp_hbm, disp),
                (radial_hbm, radial),
                (mixing_hbm, mixing),
                (readout_hbm, readout),
            )
        )
    ]
    for copy in input_copies:
        copy.start()
    own_copy = pltpu.make_async_copy(feat, win.at[2], own_sem)
    own_copy.start()
    pl.semaphore_wait(barrier, 4 + PEERS - 1)

    def columns(chunk):
        return pl.ds(pl.multiple_of(chunk * CHUNK, CHUNK), CHUNK)

    def send(chunk, slot, target, sems):
        copy = pltpu.make_async_remote_copy(
            src_ref=feat.at[:, columns(chunk)],
            dst_ref=win.at[slot, :, columns(chunk)],
            send_sem=sems,
            recv_sem=win_recv.at[slot, chunk],
            device_id={"dom": target},
            device_id_type=MESH,
        )
        copy.start()
        return copy

    even_case = 1 - odd
    first_target = jnp.where(odd == 1, at(1), at(-2))
    first_slot = jnp.where(odd == 1, 1, 4)
    second_target = jnp.where(odd == 1, at(2), at(-1))
    second_slot = jnp.where(odd == 1, 0, 3)
    whole_target = jnp.where(odd == 1, at(-2), at(2))
    whole_slot = jnp.where(odd == 1, 4, 0)
    sibling = jnp.where(odd == 1, at(-1), at(1))
    sibling_slot = jnp.where(odd == 1, 3, 1)

    copies = []
    for step in range(HALF):
        copies.append(send(step, first_slot, first_target, win_send.at[0, step]))
        copies.append(send(HALF + step, second_slot, second_target, win_send.at[0, HALF + step]))
        for chunk in (2 * step, 2 * step + 1):
            copies.append(send(chunk, whole_slot, whole_target, win_send.at[1, chunk]))
    for chunk in range(CHUNKS):
        copies.append(send(chunk, sibling_slot, sibling, win_send.at[2, chunk]))

    for copy in input_copies:
        copy.wait()

    send_read[...] = jnp.zeros_like(send_read)
    send_read[0:1, 0:CHAN] = readout[...]
    recv_read[pl.ds(my_ch, 1)] = send_read[...][None]

    def to_peers(source, landing, which):
        started = []
        for step in range(1, PEERS):
            peer = lax.rem(my_ch + step, PEERS)
            copy = pltpu.make_async_remote_copy(
                src_ref=source,
                dst_ref=landing,
                send_sem=peer_send.at[which, step],
                recv_sem=peer_recv.at[which, my_ch],
                device_id={"ch": peer},
                device_id_type=MESH,
            )
            copy.start()
            started.append(copy)
        return started

    def from_peers(landing, which):
        for step in range(1, PEERS):
            peer = lax.rem(my_ch + step, PEERS)
            pltpu.make_async_remote_copy(
                src_ref=landing(peer),
                dst_ref=landing(peer),
                send_sem=peer_send.at[which, step],
                recv_sem=peer_recv.at[which, peer],
                device_id={"ch": peer},
                device_id_type=MESH,
            ).wait_recv()

    peer_copies = to_peers(send_read, recv_read.at[my_ch], 4)

    relative = nbr[...] - ATOMS * (me - 2)
    relative = jnp.where(relative < 0, relative + count * ATOMS, relative)
    relative = jnp.where(relative >= count * ATOMS, relative - count * ATOMS, relative)
    relative = jnp.clip(relative, 0, WINDOWS * ATOMS - 1)
    lower = lax.rem(iota((SLOTS, PROBES), 1), 2) == 0
    idx_vmem[...] = relative * 4 + jnp.where(lower, PAD, PAD - 4)
    idx_copies = [
        pltpu.make_async_copy(idx_vmem.at[slot], idx[slot], idx_sem.at[slot])
        for slot in range(SLOTS)
    ]
    for copy in idx_copies:
        copy.start()

    column_comp = iota((96, 512), 1) // CHAN
    row = iota((96, 512), 0)
    spread = (lax.rem(row, 32) == column_comp) & (row < 64)
    expand[:, 0:512] = jnp.where(spread, 1.0, 0.0).astype(bf16)
    radial_rows = jnp.zeros((BASIS, 512), f32)
    comp = iota((CHAN, 512), 1) // CHAN
    same_chan = iota((CHAN, 512), 0) == lax.rem(iota((CHAN, 512), 1), CHAN)
    for degree, (first, last) in enumerate(DEGREES):
        pick = jnp.where(same_chan & (comp >= first) & (comp < last), 1.0, 0.0).astype(bf16)
        for part in split3(radial[degree]):
            radial_rows += dot(part, pick, 1, 0)
    radial_high = radial_rows.astype(bf16).astype(f32)
    radial_low = radial_rows - radial_high
    expand[:, 512:1024] = jnp.concatenate(
        [jnp.zeros((64, 512), f32), radial_high, radial_high, radial_low, radial_low], axis=0
    ).astype(bf16)

    feats[...] = jnp.zeros_like(feats)
    table[0:PAD, :] = jnp.zeros((PAD, 128), f32)
    table[TABLE_ROWS - PAD : TABLE_ROWS, :] = jnp.zeros((PAD, 128), f32)

    def weight_block(step, carry):
        slot0 = pl.multiple_of((step // 4) * 8, 8)
        probe0 = pl.multiple_of(lax.rem(step, 4) * 128, 128)
        where = (pl.ds(slot0, 8), pl.ds(probe0, 128))
        parts, radius_sq = harmonics(disp[(0,) + where], disp[(1,) + where], disp[(2,) + where])
        for comp_index, part in enumerate(parts):
            feats[8 * comp_index : 8 * comp_index + 8, :] = part
        use = mask[where].astype(f32) * (1.0 / SLOTS)
        for basis in range(BASIS):
            away = radius_sq - 0.9 * basis
            feats[256 + 8 * basis : 264 + 8 * basis, :] = jnp.exp(-(away * away)) * use
        for inner in range(8):
            values = feats[pl.ds(inner, 40, stride=8), :]
            high = values.astype(bf16).astype(f32)
            low = values - high
            left = jnp.concatenate(
                [high[0:32], low[0:32], high[32:40], low[32:40], high[32:40], low[32:40]], axis=0
            ).astype(bf16)
            base = probe0 * 4
            for pair in range(2):
                lanes = slice(256 * pair, 256 * pair + 256)
                lanes_radial = slice(512 + 256 * pair, 768 + 256 * pair)
                product = dot(left, expand[:, lanes], 0, 0) * dot(
                    left, expand[:, lanes_radial], 0, 0
                )
                for part in range(2):
                    weights[slot0 + inner, pl.ds(base + 2 * pair + part, 128, stride=4), :] = product[
                        :, 128 * part : 128 * part + 128
                    ]
        return carry

    lax.fori_loop(0, 16, weight_block, 0)

    eye = jnp.where(iota((CHUNK, CHUNK), 0) == iota((CHUNK, CHUNK), 1), 1.0, 0.0).astype(bf16)

    def to_table(slot, chunk):
        base = PAD + (slot * ATOMS + chunk * CHUNK) * 4
        for part in range(4):
            if part < 3:
                block = win[slot, 128 * part : 128 * part + 128, columns(chunk)]
            else:
                block = jnp.concatenate(
                    [win[slot, 384:400, columns(chunk)], jnp.zeros((112, CHUNK), bf16)], axis=0
                )
            table[pl.ds(base + part, CHUNK, stride=4), :] = dot(eye, block, 1, 1)

    def arrived(slot, chunk):
        pltpu.make_async_remote_copy(
            src_ref=win.at[slot, :, columns(chunk)],
            dst_ref=win.at[slot, :, columns(chunk)],
            send_sem=fwd_send.at[0, 0],
            recv_sem=win_recv.at[slot, chunk],
            device_id={"dom": sibling},
            device_id_type=MESH,
        ).wait_recv()

    def forward(chunk, slot_here, slot_there, which, step):
        copy = pltpu.make_async_remote_copy(
            src_ref=win.at[slot_here, :, columns(chunk)],
            dst_ref=win.at[slot_there, :, columns(chunk)],
            send_sem=fwd_send.at[which, step],
            recv_sem=win_recv.at[slot_there, chunk],
            device_id={"dom": sibling},
            device_id_type=MESH,
        )
        copy.start()
        return copy

    own_copy.wait()

    def own_chunk(chunk, carry):
        to_table(2, chunk)
        return carry

    lax.fori_loop(0, CHUNKS, own_chunk, 0)

    def sibling_chunk(chunk, carry):
        arrived(4 - sibling_slot, chunk)
        to_table(4 - sibling_slot, chunk)
        return carry

    lax.fori_loop(0, CHUNKS, sibling_chunk, 0)

    left_here = jnp.where(odd == 1, 0, 1)
    left_there = 1 - left_here
    right_here = jnp.where(odd == 1, 3, 4)
    right_there = 7 - right_here
    whole_here = jnp.where(odd == 1, 4, 0)

    def shared_step(step, carry):
        direct = odd * HALF + step
        arrived(left_here, direct)
        forward(direct, left_here, left_there, 0, step)
        arrived(right_here, direct)
        forward(direct, right_here, right_there, 1, step)
        to_table(left_here, direct)
        to_table(right_here, direct)
        arrived(whole_here, 2 * step)
        to_table(whole_here, 2 * step)
        arrived(whole_here, 2 * step + 1)
        to_table(whole_here, 2 * step + 1)
        other = even_case * HALF + step
        arrived(left_here, other)
        to_table(left_here, other)
        arrived(right_here, other)
        to_table(right_here, other)
        return carry

    lax.fori_loop(0, HALF, shared_step, 0)

    for copy in idx_copies:
        copy.wait()
    upper_half = iota((8, 128), 0) < 4

    def probe_block(block, carry):
        for inner in range(UNROLL):
            pair = block * UNROLL + inner
            first_probe, second_probe = 2 * pair, 2 * pair + 1
            rows_at = pl.ds(pl.multiple_of(pair * 8, 8), 8)
            total = jnp.zeros((8, 128), f32)
            for slot in range(SLOTS):
                first = table[pl.ds(idx[slot][first_probe], 8), :]
                second = table[pl.ds(idx[slot][second_probe], 8), :]
                atom = jnp.where(upper_half, first, second)
                total = total + atom * weights[slot, rows_at, :]
            acc[rows_at, :] = total
        return carry

    chan_pick = jnp.where(
        iota((CHAN, 128), 0) == lax.rem(iota((CHAN, 128), 1), CHAN), 1.0, 0.0
    ).astype(bf16)
    my_rows = pl.ds(pl.multiple_of(my_ch * CHAN, CHAN), CHAN)
    blocks = 64 // UNROLL
    for group in range(4):
        lax.fori_loop(group * blocks, (group + 1) * blocks, probe_block, 0)
        summed = acc[pl.ds(512 * group, 128, stride=4), :]
        for part in range(1, 4):
            summed = summed + acc[pl.ds(512 * group + part, 128, stride=4), :]
        field = jnp.zeros((CHAN, 128), f32)
        for part in split3(summed):
            field = field + dot(chan_pick, part, 1, 1)
        field_all[group, my_rows, :] = field
        tile = field_all.at[group, my_rows, :]
        peer_copies += to_peers(tile, tile, group)

    from_peers(lambda peer: recv_read.at[peer], 4)
    read_row = jnp.zeros((8, 128), f32)
    for peer in range(PEERS):
        part = recv_read[peer]
        read_row = read_row + (part if peer == 0 else pltpu.roll(part, CHAN * peer, 1))
    read_parts = split3(read_row)
    for group in range(4):
        from_peers(
            lambda peer: field_all.at[
                group, pl.ds(pl.multiple_of(peer * CHAN, CHAN), CHAN), :
            ],
            group,
        )
        mixed = jnp.zeros((128, 128), f32)
        for part in split3(field_all[group]):
            mixed = mixed + dot(mixing[...], part, 0, 0)
        active = split3(mixed / (1.0 + jnp.exp(-mixed)))
        dens = jnp.zeros((8, 128), f32)
        for left_part, right_part in ((0, 0), (0, 1), (1, 0), (1, 1), (0, 2), (2, 0)):
            dens = dens + dot(read_parts[left_part], active[right_part], 1, 0)
        out[0:1, 128 * group : 128 * group + 128] = dens[0:1]

    for copy in copies + peer_copies:
        copy.wait_send()

    def forwarded(step, carry):
        for which in range(2):
            pltpu.make_async_remote_copy(
                src_ref=win.at[0, :, columns(0)],
                dst_ref=win.at[0, :, columns(0)],
                send_sem=fwd_send.at[which, step],
                recv_sem=win_recv.at[0, 0],
                device_id={"dom": sibling},
                device_id_type=MESH,
            ).wait_send()
        return carry

    lax.fori_loop(0, HALF, forwarded, 0)


def per_device(feat, nbr, mask, disp, radial, mixing, readout):
    vmem = pl.BlockSpec(memory_space=pltpu.VMEM)
    dma = pltpu.SemaphoreType.DMA
    tile = (8, 128)
    density = pl.pallas_call(
        kernel,
        out_shape=jax.ShapeDtypeStruct((1, PROBES), f32),
        in_specs=[pl.BlockSpec(memory_space=pl.ANY)] * 7,
        out_specs=vmem,
        scratch_shapes=[
            pltpu.VMEM((SLOTS, PROBES), jnp.int32),
            pltpu.VMEM((SLOTS, PROBES), jnp.int32),
            pltpu.VMEM((3, SLOTS, PROBES), f32),
            pltpu.VMEM((5, BASIS, CHAN), f32),
            pltpu.VMEM((128, 128), bf16),
            pltpu.VMEM((1, CHAN), f32),
            pltpu.VMEM((WINDOWS, ROWS, ATOMS), bf16),
            pltpu.VMEM((TABLE_ROWS, 128), f32),
            pltpu.VMEM((SLOTS, SLOT_ROWS, 128), f32),
            pltpu.VMEM((SLOT_ROWS, 128), f32),
            pltpu.VMEM((320, 128), f32),
            pltpu.VMEM((96, 1024), bf16),
            pltpu.VMEM((SLOTS, PROBES), jnp.int32),
            pltpu.VMEM((4, 128, 128), f32),
            pltpu.VMEM(tile, f32),
            pltpu.VMEM((PEERS,) + tile, f32),
            dma((6,)),
            dma((3, CHUNKS)),
            dma((WINDOWS, CHUNKS)),
            dma((2, HALF)),
            dma,
            dma((SLOTS,)),
            dma((5, PEERS)),
            dma((5, PEERS)),
        ]
        + [pltpu.SMEM((PROBES,), jnp.int32)] * SLOTS,
        compiler_params=pltpu.CompilerParams(
            collective_id=0, has_side_effects=True, vmem_limit_bytes=64 * 1024 * 1024 - 65536
        ),
    )(
        feat.reshape(ROWS, ATOMS),
        nbr,
        mask,
        disp,
        radial.transpose(1, 0, 2),
        mixing,
        readout.reshape(1, CHAN),
    )
    return density.reshape(PROBES)


def solution(mesh):
    return jax.shard_map(
        per_device,
        mesh=mesh,
        in_specs=(
            P(None, "ch", "dom"),
            P(None, "dom"),
            P(None, "dom"),
            P(None, None, "dom"),
            P(None, None, "ch"),
            P(),
            P("ch"),
        ),
        out_specs=P("dom"),
        check_vma=False,
    )
```

time: 307 us -> 64.9 us (0.21)
  the two profiles are of different devices: /device:TPU:2 before, /device:TPU:1 now
where the time goes in v1:
time: 64.9 us; the launch traced here: 64.8 us
  Pallas kernels  63.5 us (98%)
  local copies, waits for them, and re-layouts  1.26 us (2%)
    pallas_call x1, Pallas kernels, per_device(): pl.pallas_call(kernel, out_shape=jax.ShapeDtypeStruct((1, PROBES), f32),...  63.5 us

profile of v1, /device:TPU:1, one launch (start us, length us, event | category | flops | bytes accessed | tf_op | source)
XLA Modules:
  0.0 64.8 jit_solution(1340511041000894923)
XLA Ops:
  0.0 63.5 %shard_map.73 = f32[1,512]{1,0:T(1,128)} custom-call(bf16[400,1536]{1,0:T(8,128)(2,1)} %bitcast.4, s32[32,512]{1,0:T(8,128)} %nbr_hbm.1, s32[32,512]{1,0:T(8,128)} %mask_hbm.1, f32[3,32,512]{2,1,0:T(8,128)} %disp_hbm.1, f32[5,8,16]{2,1,0:T(8,128)} %bitcast.5, bf16[128,128]{1,0:T(8,128)(2,1)} %mixing_hbm.1, f32[1,16]{1,0:T(1,128)} %bitcast.7), custom_call_target="tpu_custom_call" | custom-call | tf_op jit(solution)/shard_map/pallas_call | solution.py:449
  63.5 1.3 %copy.9 = f32[512]{0:T(512)} copy(f32[512]{0:T(512)} %bitcast.6) | data formatting | bytes 4096

commit v2 on v1

--- a/solution.py
+++ b/solution.py
@@ -15,13 +15,14 @@
 SLOTS = 32
 BASIS = 8
 WINDOWS = 5
-CHUNK = 256
+CHUNK = 128
 CHUNKS = ATOMS // CHUNK
 HALF = CHUNKS // 2
 PAD = 4
 TABLE_ROWS = PAD + WINDOWS * ATOMS * 4 + PAD
 SLOT_ROWS = PROBES * 4
 PEERS = 8
+FAR_FIRST = (4, 3, 5, 2, 6, 1, 7)
 UNROLL = 4
 DEGREES = ((0, 1), (1, 4), (4, 9), (9, 16), (16, 25))
 MESH = pl.DeviceIdType.MESH
@@ -129,7 +130,7 @@
     barrier = pltpu.get_barrier_semaphore()
     for offset in (-2, -1, 1, 2):
         pl.semaphore_signal(barrier, inc=1, device_id={"dom": at(offset)}, device_id_type=MESH)
-    for step in range(1, PEERS):
+    for step in FAR_FIRST:
         peer = lax.rem(my_ch + step, PEERS)
         pl.semaphore_signal(barrier, inc=1, device_id={"ch": peer}, device_id_type=MESH)
 
@@ -181,8 +182,6 @@
     for step in range(HALF):
         copies.append(send(step, first_slot, first_target, win_send.at[0, step]))
         copies.append(send(HALF + step, second_slot, second_target, win_send.at[0, HALF + step]))
-        for chunk in (2 * step, 2 * step + 1):
-            copies.append(send(chunk, whole_slot, whole_target, win_send.at[1, chunk]))
     for chunk in range(CHUNKS):
         copies.append(send(chunk, sibling_slot, sibling, win_send.at[2, chunk]))
 
@@ -195,7 +194,7 @@
 
     def to_peers(source, landing, which):
         started = []
-        for step in range(1, PEERS):
+        for step in FAR_FIRST:
             peer = lax.rem(my_ch + step, PEERS)
             copy = pltpu.make_async_remote_copy(
                 src_ref=source,
@@ -288,7 +287,12 @@
                     ]
         return carry
 
-    lax.fori_loop(0, 16, weight_block, 0)
+    lax.fori_loop(0, 6, weight_block, 0)
+
+    for chunk in range(CHUNKS):
+        copies.append(send(chunk, whole_slot, whole_target, win_send.at[1, chunk]))
+
+    lax.fori_loop(6, 16, weight_block, 0)
 
     eye = jnp.where(iota((CHUNK, CHUNK), 0) == iota((CHUNK, CHUNK), 1), 1.0, 0.0).astype(bf16)
 
@@ -354,10 +358,6 @@
         forward(direct, right_here, right_there, 1, step)
         to_table(left_here, direct)
         to_table(right_here, direct)
-        arrived(whole_here, 2 * step)
-        to_table(whole_here, 2 * step)
-        arrived(whole_here, 2 * step + 1)
-        to_table(whole_here, 2 * step + 1)
         other = even_case * HALF + step
         arrived(left_here, other)
         to_table(left_here, other)
@@ -366,6 +366,13 @@
         return carry
 
     lax.fori_loop(0, HALF, shared_step, 0)
+
+    def whole_step(chunk, carry):
+        arrived(whole_here, chunk)
+        to_table(whole_here, chunk)
+        return carry
+
+    lax.fori_loop(0, CHUNKS, whole_step, 0)
 
     for copy in idx_copies:
         copy.wait()
@@ -390,17 +397,54 @@
     ).astype(bf16)
     my_rows = pl.ds(pl.multiple_of(my_ch * CHAN, CHAN), CHAN)
     blocks = 64 // UNROLL
-    for group in range(4):
+
+    def probe_group(group, carry):
         lax.fori_loop(group * blocks, (group + 1) * blocks, probe_block, 0)
-        summed = acc[pl.ds(512 * group, 128, stride=4), :]
+        start = group * 512
+        summed = acc[pl.ds(start, 128, stride=4), :]
         for part in range(1, 4):
-            summed = summed + acc[pl.ds(512 * group + part, 128, stride=4), :]
+            summed = summed + acc[pl.ds(start + part, 128, stride=4), :]
         field = jnp.zeros((CHAN, 128), f32)
         for part in split3(summed):
             field = field + dot(chan_pick, part, 1, 1)
         field_all[group, my_rows, :] = field
         tile = field_all.at[group, my_rows, :]
-        peer_copies += to_peers(tile, tile, group)
+        to_peers(tile, tile, group)
+        return carry
+
+    lax.fori_loop(0, 4, probe_group, 0)
+
+    for copy in copies + peer_copies:
+        copy.wait_send()
+
+    def forwarded(step, carry):
+        for which in range(2):
+            pltpu.make_async_remote_copy(
+                src_ref=win.at[0, :, columns(0)],
+                dst_ref=win.at[0, :, columns(0)],
+                send_sem=fwd_send.at[which, step],
+                recv_sem=win_recv.at[0, 0],
+                device_id={"dom": sibling},
+                device_id_type=MESH,
+            ).wait_send()
+        return carry
+
+    lax.fori_loop(0, HALF, forwarded, 0)
+
+    def sent(group, carry):
+        tile = field_all.at[group, my_rows, :]
+        for step in range(1, PEERS):
+            pltpu.make_async_remote_copy(
+                src_ref=tile,
+                dst_ref=tile,
+                send_sem=peer_send.at[group, step],
+                recv_sem=peer_recv.at[group, my_ch],
+                device_id={"ch": lax.rem(my_ch + step, PEERS)},
+                device_id_type=MESH,
+            ).wait_send()
+        return carry
+
+    lax.fori_loop(0, 4, sent, 0)
 
     from_peers(lambda peer: recv_read.at[peer], 4)
     read_row = jnp.zeros((8, 128), f32)
@@ -423,23 +467,6 @@
         for left_part, right_part in ((0, 0), (0, 1), (1, 0), (1, 1), (0, 2), (2, 0)):
             dens = dens + dot(read_parts[left_part], active[right_part], 1, 0)
         out[0:1, 128 * group : 128 * group + 128] = dens[0:1]
-
-    for copy in copies + peer_copies:
-        copy.wait_send()
-
-    def forwarded(step, carry):
-        for which in range(2):
-            pltpu.make_async_remote_copy(
-                src_ref=win.at[0, :, columns(0)],
-                dst_ref=win.at[0, :, columns(0)],
-                send_sem=fwd_send.at[which, step],
-                recv_sem=win_recv.at[0, 0],
-                device_id={"dom": sibling},
-                device_id_type=MESH,
-            ).wait_send()
-        return carry
-
-    lax.fori_loop(0, HALF, forwarded, 0)
 
 
 def per_device(feat, nbr, mask, disp, radial, mixing, readout):

time: 64.9 us -> 63.1 us (0.972)
  Pallas kernels: 63.5 us -> 61.7 us
    pallas_call x1, Pallas kernels: 63.5 us -> 61.7 us  [per_device(): pl.pallas_call(kernel, out_shape=jax.ShapeDtypeStruct((1, PROBES), f32),...]
where the time goes in v2:
time: 63.1 us; the launch traced here: 63 us
  Pallas kernels  61.7 us (98%)
  local copies, waits for them, and re-layouts  1.26 us (2%)
    pallas_call x1, Pallas kernels, per_device(): pl.pallas_call(kernel, out_shape=jax.ShapeDtypeStruct((1, PROBES), f32),...  61.7 us

profile of v2, /device:TPU:1, one launch (start us, length us, event | category | flops | bytes accessed | tf_op | source)
XLA Modules:
  0.0 63.0 jit_solution(8986156765973973857)
XLA Ops:
  0.0 61.7 %shard_map.73 = f32[1,512]{1,0:T(1,128)} custom-call(bf16[400,1536]{1,0:T(8,128)(2,1)} %bitcast.4, s32[32,512]{1,0:T(8,128)} %nbr_hbm.1, s32[32,512]{1,0:T(8,128)} %mask_hbm.1, f32[3,32,512]{2,1,0:T(8,128)} %disp_hbm.1, f32[5,8,16]{2,1,0:T(8,128)} %bitcast.5, bf16[128,128]{1,0:T(8,128)(2,1)} %mixing_hbm.1, f32[1,16]{1,0:T(1,128)} %bitcast.7), custom_call_target="tpu_custom_call" | custom-call | tf_op jit(solution)/shard_map/pallas_call | solution.py:476
  61.7 1.3 %copy.9 = f32[512]{0:T(512)} copy(f32[512]{0:T(512)} %bitcast.6) | data formatting | bytes 4096

commit v3 on v2

--- a/solution.py
+++ b/solution.py
@@ -17,7 +17,6 @@
 WINDOWS = 5
 CHUNK = 128
 CHUNKS = ATOMS // CHUNK
-HALF = CHUNKS // 2
 PAD = 4
 TABLE_ROWS = PAD + WINDOWS * ATOMS * 4 + PAD
 SLOT_ROWS = PROBES * 4
@@ -168,20 +167,16 @@
         copy.start()
         return copy
 
-    even_case = 1 - odd
-    first_target = jnp.where(odd == 1, at(1), at(-2))
-    first_slot = jnp.where(odd == 1, 1, 4)
-    second_target = jnp.where(odd == 1, at(2), at(-1))
-    second_slot = jnp.where(odd == 1, 0, 3)
+    shared_target = jnp.where(odd == 1, at(2), at(-2))
+    shared_slot = jnp.where(odd == 1, 0, 4)
     whole_target = jnp.where(odd == 1, at(-2), at(2))
     whole_slot = jnp.where(odd == 1, 4, 0)
     sibling = jnp.where(odd == 1, at(-1), at(1))
     sibling_slot = jnp.where(odd == 1, 3, 1)
 
     copies = []
-    for step in range(HALF):
-        copies.append(send(step, first_slot, first_target, win_send.at[0, step]))
-        copies.append(send(HALF + step, second_slot, second_target, win_send.at[0, HALF + step]))
+    for chunk in range(CHUNKS):
+        copies.append(send(chunk, shared_slot, shared_target, win_send.at[0, chunk]))
     for chunk in range(CHUNKS):
         copies.append(send(chunk, sibling_slot, sibling, win_send.at[2, chunk]))
 
@@ -287,12 +282,12 @@
                     ]
         return carry
 
-    lax.fori_loop(0, 6, weight_block, 0)
+    lax.fori_loop(0, 8, weight_block, 0)
 
     for chunk in range(CHUNKS):
         copies.append(send(chunk, whole_slot, whole_target, win_send.at[1, chunk]))
 
-    lax.fori_loop(6, 16, weight_block, 0)
+    lax.fori_loop(8, 16, weight_block, 0)
 
     eye = jnp.where(iota((CHUNK, CHUNK), 0) == iota((CHUNK, CHUNK), 1), 1.0, 0.0).astype(bf16)
 
@@ -311,17 +306,17 @@
         pltpu.make_async_remote_copy(
             src_ref=win.at[slot, :, columns(chunk)],
             dst_ref=win.at[slot, :, columns(chunk)],
-            send_sem=fwd_send.at[0, 0],
+            send_sem=fwd_send.at[0],
             recv_sem=win_recv.at[slot, chunk],
             device_id={"dom": sibling},
             device_id_type=MESH,
         ).wait_recv()
 
-    def forward(chunk, slot_here, slot_there, which, step):
+    def forward(chunk, slot_here, slot_there):
         copy = pltpu.make_async_remote_copy(
             src_ref=win.at[slot_here, :, columns(chunk)],
             dst_ref=win.at[slot_there, :, columns(chunk)],
-            send_sem=fwd_send.at[which, step],
+            send_sem=fwd_send.at[chunk],
             recv_sem=win_recv.at[slot_there, chunk],
             device_id={"dom": sibling},
             device_id_type=MESH,
@@ -344,28 +339,24 @@
 
     lax.fori_loop(0, CHUNKS, sibling_chunk, 0)
 
-    left_here = jnp.where(odd == 1, 0, 1)
-    left_there = 1 - left_here
-    right_here = jnp.where(odd == 1, 3, 4)
-    right_there = 7 - right_here
+    handed_slot = jnp.where(odd == 1, 1, 3)
+    gotten_slot = jnp.where(odd == 1, 3, 1)
     whole_here = jnp.where(odd == 1, 4, 0)
 
-    def shared_step(step, carry):
-        direct = odd * HALF + step
-        arrived(left_here, direct)
-        forward(direct, left_here, left_there, 0, step)
-        arrived(right_here, direct)
-        forward(direct, right_here, right_there, 1, step)
-        to_table(left_here, direct)
-        to_table(right_here, direct)
-        other = even_case * HALF + step
-        arrived(left_here, other)
-        to_table(left_here, other)
-        arrived(right_here, other)
-        to_table(right_here, other)
-        return carry
-
-    lax.fori_loop(0, HALF, shared_step, 0)
+    def shared_step(chunk, carry):
+        arrived(shared_slot, chunk)
+        forward(chunk, shared_slot, handed_slot)
+        to_table(shared_slot, chunk)
+        return carry
+
+    lax.fori_loop(0, CHUNKS, shared_step, 0)
+
+    def gotten_step(chunk, carry):
+        arrived(gotten_slot, chunk)
+        to_table(gotten_slot, chunk)
+        return carry
+
+    lax.fori_loop(0, CHUNKS, gotten_step, 0)
 
     def whole_step(chunk, carry):
         arrived(whole_here, chunk)
@@ -417,19 +408,18 @@
     for copy in copies + peer_copies:
         copy.wait_send()
 
-    def forwarded(step, carry):
-        for which in range(2):
-            pltpu.make_async_remote_copy(
-                src_ref=win.at[0, :, columns(0)],
-                dst_ref=win.at[0, :, columns(0)],
-                send_sem=fwd_send.at[which, step],
-                recv_sem=win_recv.at[0, 0],
-                device_id={"dom": sibling},
-                device_id_type=MESH,
-            ).wait_send()
-        return carry
-
-    lax.fori_loop(0, HALF, forwarded, 0)
+    def forwarded(chunk, carry):
+        pltpu.make_async_remote_copy(
+            src_ref=win.at[0, :, columns(0)],
+            dst_ref=win.at[0, :, columns(0)],
+            send_sem=fwd_send.at[chunk],
+            recv_sem=win_recv.at[0, 0],
+            device_id={"dom": sibling},
+            device_id_type=MESH,
+        ).wait_send()
+        return carry
+
+    lax.fori_loop(0, CHUNKS, forwarded, 0)
 
     def sent(group, carry):
         tile = field_all.at[group, my_rows, :]
@@ -498,7 +488,7 @@
             dma((6,)),
             dma((3, CHUNKS)),
             dma((WINDOWS, CHUNKS)),
-            dma((2, HALF)),
+            dma((CHUNKS,)),
             dma,
             dma((SLOTS,)),
             dma((5, PEERS)),

time: 63.1 us -> 62.8 us (level)
  Pallas kernels: 61.7 us -> 60.9 us
    pallas_call x1, Pallas kernels: 61.7 us -> 60.9 us  [per_device(): pl.pallas_call(kernel, out_shape=jax.ShapeDtypeStruct((1, PROBES), f32),...]
where the time goes in v3:
time: 62.8 us; the launch traced here: 62.2 us
  Pallas kernels  60.9 us (97%)
  local copies, waits for them, and re-layouts  1.26 us (2%)
    pallas_call x1, Pallas kernels, per_device(): pl.pallas_call(kernel, out_shape=jax.ShapeDtypeStruct((1, PROBES), f32),...  60.9 us
    unnamed x1, local copies, waits for them, and re-layouts  1.26 us

profile of v3, /device:TPU:1, one launch (start us, length us, event | category | flops | bytes accessed | tf_op | source)
XLA Modules:
  0.0 62.2 jit_solution(16851334667469079414)
XLA Ops:
  0.0 60.9 %shard_map.73 = f32[1,512]{1,0:T(1,128)} custom-call(bf16[400,1536]{1,0:T(8,128)(2,1)} %bitcast.4, s32[32,512]{1,0:T(8,128)} %nbr_hbm.1, s32[32,512]{1,0:T(8,128)} %mask_hbm.1, f32[3,32,512]{2,1,0:T(8,128)} %disp_hbm.1, f32[5,8,16]{2,1,0:T(8,128)} %bitcast.5, bf16[128,128]{1,0:T(8,128)(2,1)} %mixing_hbm.1, f32[1,16]{1,0:T(1,128)} %bitcast.7), custom_call_target="tpu_custom_call" | custom-call | tf_op jit(solution)/shard_map/pallas_call | solution.py:466
  61.0 1.3 %copy.9 = f32[512]{0:T(512)} copy(f32[512]{0:T(512)} %bitcast.6) | data formatting | bytes 4096
